TPU v7x, 32 devices: a whole 2x2x4 slice. The times are simulated.
32 devices in a mesh: sub: 8 (over z, y), mode: 4 (over x, core).
Axes of the slice: x: 2, y: 2, z: 4, core: 2. Of those that a mesh axis runs over, the one named last changes fastest.
Arguments:
- panels: bfloat16 [8, 2048, 768], P('sub', 'mode'), may hold values from -0.59765625 to 0.59765625
- eigvals: float32 [8, 2048], P('sub', 'mode'), may hold values from 0.5 to 20
- counts: int32 [8], P('sub'), may hold values from 512 to 2048, as said below
- separator_diag: float32 [8, 768], P('sub'), may hold values from 4 to 8
- separator_index_tables: int32 [8, 768], replicated, may hold values from 0 to 767, each once within a row
Outputs:
- condensed: float32 [768, 768], P('sub')
Inputs may be any that keep to these rules, and one draw needn't show every extreme that they name: `counts`: every value from 512 to 2048 can occur, and both ends occur in every draw. `separator_index_tables`: each row is a permutation of 0 to 767.
All inputs are finite; a program needn't handle non-finite values.
Results may differ from a plain program's by a relative error of at most 0.0003.
Values sent between devices are 32-bit elements; how exact they have to be, the bound alone decides.
A program may use at most 64 MiB of HBM per device.

v0:
```python
import math

import jax
import jax.numpy as jnp
from jax import lax
from jax.sharding import PartitionSpec as P


def from_partner(array, axis, stride):
    return lax.ppermute(array, axis, [(i, i ^ 1 << stride) for i in range(lax.axis_size(axis))])


def select_permutation(separator_index_tables, level_number, tree_node_index):
    span_rows = 2**level_number
    map_row = tree_node_index * span_rows + span_rows - 1
    base_perm = lax.dynamic_index_in_dim(separator_index_tables, map_row, 0, keepdims=False)
    sep_width = separator_index_tables.shape[1]
    shifted = (jnp.arange(sep_width, dtype=jnp.int32) + 97 * level_number % sep_width) % sep_width
    return jnp.take(base_perm, shifted)


def relabel_equations(schur_remainder_patch, arrangement_list):
    rows_first = jnp.take(schur_remainder_patch, arrangement_list, axis=0)
    return jnp.take(rows_first.T, arrangement_list, axis=0).T


def local(panels, eigvals, counts, separator_diag, separator_index_tables):
    sub_here = lax.axis_index("sub")
    mode_here = lax.axis_index("mode")
    sub_dev = panels.shape[0]
    mode_dev = panels.shape[1]
    sep_width = panels.shape[2]
    mode_start = mode_here * mode_dev
    diag_on = (mode_here == 0).astype(jnp.float32)
    contract = (((0,), (0,)), ((), ()))
    first_leaf = sub_here * sub_dev
    stack_nodes = []
    panel_rows = panels[0]
    live_count = counts[0]
    live_mask = (mode_start + jnp.arange(mode_dev, dtype=jnp.int32) < live_count).astype(
        jnp.float32
    )
    weighted = (panel_rows.astype(jnp.float32) * (live_mask / eigvals[0])[:, None]).astype(
        jnp.bfloat16
    )
    partial_sum = lax.dot_general(
        weighted, panel_rows, contract, preferred_element_type=jnp.float32
    )
    stack_nodes.append((0, diag_on * jnp.diag(separator_diag[0]) - partial_sum))
    while len(stack_nodes) >= 2 and stack_nodes[-1][0] == stack_nodes[-2][0]:
        level_number, right_matrix_tile = stack_nodes.pop()
        level_same, left_matrix_tile = stack_nodes.pop()
        span_leaves = 2 ** (level_number + 1)
        left_child_node = first_leaf // 2**level_number + 2 * ((1 - span_leaves) // span_leaves)
        reordered_first_factor = relabel_equations(
            left_matrix_tile,
            select_permutation(separator_index_tables, level_number, left_child_node),
        )
        reordered_second_factor = relabel_equations(
            right_matrix_tile,
            select_permutation(separator_index_tables, level_number, left_child_node + 1),
        )
        stack_nodes.append((level_number + 1, reordered_first_factor + reordered_second_factor))
    device_level_count, schur_remainder_patch = stack_nodes[0]
    sub_count = lax.axis_size("sub")
    sub_bits = sub_count.bit_length() - 1
    schur_remainder_patch = lax.psum(schur_remainder_patch, "mode")
    for bit_position in range(sub_bits):
        tree_node_index = sub_here // 2**bit_position
        schur_remainder_patch = relabel_equations(
            schur_remainder_patch,
            select_permutation(
                separator_index_tables, device_level_count + bit_position, tree_node_index
            ),
        )
        schur_remainder_patch = schur_remainder_patch + from_partner(
            schur_remainder_patch, "sub", bit_position
        )
    own_rows = sep_width // sub_count
    own_block = lax.dynamic_slice_in_dim(schur_remainder_patch, sub_here * own_rows, own_rows, 0)
    return own_block * (1.0 / math.sqrt(sub_dev * sub_count))


def solution(mesh):
    return jax.shard_map(
        local,
        mesh=mesh,
        in_specs=(P("sub", "mode", None), P("sub", "mode"), P("sub"), P("sub", None), P()),
        out_specs=P("sub", None),
        check_vma=False,
    )
```

profile of v0, /device:TPU:0, one launch (start us, length us, event | category | flops | bytes accessed | tf_op | source)
XLA Modules:
  0.0 345.9 jit_solution(12305404054721332280)
XLA Ops:
  6.5 0.0 all-reduce.2.cloned.1.call-start
  7.2 0.7 reduce.3
  7.9 0.7 convert_divide_fusion
  8.6 3.7 %multiply_subtract_fusion = f32[768,768]{1,0:T(8,128)} fusion(f32[768]{0:T(1024)S(1)} %reduce.3, f32[]{:T(128)S(6)} %convert_element_type.20, bf16[1,512,768]{2,1,0:T(8,128)(2,1)} %param.9, f32[512]{0:T(512)S(1)} %convert_divide_fusion), kind=kOutput, calls=%fused_computation.15 | convolution fusion | flops 607518720 | bytes 3150852 | tf_op jit(solution)/shard_map/dot_general | solution.py:46
  12.3 0.0 all-reduce.2.cloned.1.call-update
  12.4 0.9 dynamic-slice_reduce_fusion
  13.3 3.2 gather_fusion
  16.5 54.3 %all-reduce.2.cloned.1.call-done = f32[768,768]{1,0:T(8,128)} async-done(((f32[768,768]{1,0:T(8,128)}), f32[768,768]{1,0:T(8,128)}) %all-reduce.2.cloned.1.call-update) | async-done | bytes 2359312 | tf_op jit(solution)/shard_map/psum | solution.py:67
  70.8 5.1 %gather_fusion.1 = f32[768,768]{1,0:T(8,128)S(1)} fusion(f32[768,768]{1,0:T(8,128)} %all-reduce.2.cloned.1.call-done, s32[1024]{0:T(1024)S(1)} %pad_clamp_fusion.2), kind=kCustom, calls=%fused_computation.1.clone | custom fusion | bytes 4721664 | tf_op jit(solution)/shard_map/jit(_take)/gather | solution.py:23
  76.0 1.6 select_bitcast_fusion.5
  77.6 2.0 copy.18
  79.7 3.5 %gather_fusion.2 = f32[768,768]{1,0:T(8,128)} fusion(f32[768,768]{1,0:T(8,128)S(1)} %copy.18, s32[1024]{0:T(1024)S(1)} %pad_clamp_fusion.2), kind=kCustom, calls=%fused_computation.4.clone | custom fusion | bytes 4721664 | tf_op jit(solution)/shard_map/jit(_take)/gather | solution.py:24
  83.1 3.3 select_bitcast_fusion.4
  86.5 0.0 copy-start.1
  86.5 1.5 collective-permute-start
  88.0 3.2 gather_fusion.3
  91.2 48.5 %collective-permute-done = f32[768,768]{0,1:T(8,128)} collective-permute-done((f32[768,768]{0,1:T(8,128)}, f32[768,768]{0,1:T(8,128)}, u32[]{:S(2)}, u32[]{:S(2)}) %collective-permute-start) | collective-permute-done | bytes 2359328 | tf_op jit(solution)/shard_map/ppermute | solution.py:10
  139.7 0.0 copy-done.1
  139.7 3.5 %fusion.12 = f32[768,768]{0,1:T(8,128)} fusion(f32[768,768]{0,1:T(8,128)} %collective-permute-done, f32[768,768]{1,0:T(8,128)S(1)} %copy-done.1, pred[768]{0:T(1024)(128)(4,1)S(1)} %compare_and_fusion.2), kind=kLoop, calls=%fused_computation.53 | loop fusion | flops 1179648 | bytes 7078656 | tf_op jit(solution)/shard_map/add | solution.py:76
  143.2 2.0 copy.19
  145.2 3.5 %gather_fusion.4 = f32[768,768]{1,0:T(8,128)} fusion(f32[768,768]{1,0:T(8,128)S(1)} %copy.19, s32[1024]{0:T(1024)S(1)} %pad_clamp_fusion.1), kind=kCustom, calls=%fused_computation.5.clone | custom fusion | bytes 4721664 | tf_op jit(solution)/shard_map/jit(_take)/gather | solution.py:23
  148.7 3.3 select_bitcast_fusion.3
  152.0 2.0 copy.20
  154.0 3.5 %gather_fusion.5 = f32[768,768]{1,0:T(8,128)} fusion(f32[768,768]{1,0:T(8,128)S(1)} %copy.20, s32[1024]{0:T(1024)S(1)} %pad_clamp_fusion.1), kind=kCustom, calls=%fused_computation.6.clone | custom fusion | bytes 4721664 | tf_op jit(solution)/shard_map/jit(_take)/gather | solution.py:24
  157.5 3.3 select_bitcast_fusion.2
  160.8 0.0 copy-start
  160.8 1.5 collective-permute-start.1
  162.3 3.2 gather_fusion.6
  165.6 47.6 %collective-permute-done.1 = f32[768,768]{0,1:T(8,128)} collective-permute-done((f32[768,768]{0,1:T(8,128)}, f32[768,768]{0,1:T(8,128)}, u32[]{:S(2)}, u32[]{:S(2)}) %collective-permute-start.1) | collective-permute-done | bytes 2359328 | tf_op jit(solution)/shard_map/ppermute | solution.py:10
  213.2 0.0 copy-done
  213.2 3.4 fusion.11
  216.6 2.0 copy.21
  218.6 3.5 %gather_fusion.7 = f32[768,768]{1,0:T(8,128)} fusion(f32[768,768]{1,0:T(8,128)S(1)} %copy.21, s32[1024]{0:T(1024)S(1)} %pad_clamp_fusion), kind=kCustom, calls=%fused_computation.7.clone | custom fusion | bytes 4721664 | tf_op jit(solution)/shard_map/jit(_take)/gather | solution.py:23
  222.1 3.3 select_bitcast_fusion.1
  225.4 2.0 copy.22
  227.5 3.5 %gather_fusion.8 = f32[768,768]{1,0:T(8,128)} fusion(f32[768,768]{1,0:T(8,128)S(1)} %copy.22, s32[1024]{0:T(1024)S(1)} %pad_clamp_fusion), kind=kCustom, calls=%fused_computation.8.clone | custom fusion | bytes 4721664 | tf_op jit(solution)/shard_map/jit(_take)/gather | solution.py:24
  230.9 2.0 copy.23
  233.0 1.6 select_bitcast_fusion
  234.5 2.4 collective-permute-start.2
  236.9 100.4 %collective-permute-done.2 = f32[768,768]{1,0:T(8,128)S(1)} collective-permute-done((f32[768,768]{1,0:T(8,128)}, f32[768,768]{1,0:T(8,128)S(1)}, u32[]{:S(2)}, u32[]{:S(2)}) %collective-permute-start.2) | collective-permute-done | bytes 2359328 | tf_op jit(solution)/shard_map/ppermute | solution.py:10
  337.3 1.7 fusion.4
  (15 shorter events, 0.1 us)
Async XLA Ops:
  6.5 64.3 %all-reduce.2.cloned.1.call-start = ((), (), s32[]{:S(2)}) async-start(), calls=%async_computation | async-start | bytes 4718592 | tf_op jit(solution)/shard_map/psum | solution.py:67
  86.5 53.2 %copy-start.1 = (f32[768,768]{1,0:T(8,128)S(1)}, f32[768,768]{1,0:T(8,128)}, u32[]{:S(2)}) copy-start(f32[768,768]{1,0:T(8,128)} %gather_fusion.2) | copy-start | bytes 7077892
  86.5 53.2 %collective-permute-start = (f32[768,768]{0,1:T(8,128)}, f32[768,768]{0,1:T(8,128)}, u32[]{:S(2)}, u32[]{:S(2)}) collective-permute-start(f32[768,768]{0,1:T(8,128)} %select_bitcast_fusion.4), channel_id=1, source_target_pairs={{0,4},{4,0},{8,12},{12,8},{16,20},{20,16},{24,28},{28,24},{1,5},{5... | collective-permute-start | bytes 7077896 | tf_op jit(solution)/shard_map/ppermute | solution.py:10
  160.8 52.3 %copy-start = (f32[768,768]{1,0:T(8,128)S(1)}, f32[768,768]{1,0:T(8,128)}, u32[]{:S(2)}) copy-start(f32[768,768]{1,0:T(8,128)} %gather_fusion.5) | copy-start | bytes 7077892
  160.8 52.3 %collective-permute-start.1 = (f32[768,768]{0,1:T(8,128)}, f32[768,768]{0,1:T(8,128)}, u32[]{:S(2)}, u32[]{:S(2)}) collective-permute-start(f32[768,768]{0,1:T(8,128)} %select_bitcast_fusion.2), channel_id=1, source_target_pairs={{0,8},{4,12},{8,0},{12,4},{16,24},{20,28},{24,16},{28,20},{1,9},{5... | collective-permute-start | bytes 7077896 | tf_op jit(solution)/shard_map/ppermute | solution.py:10
  234.5 102.8 %collective-permute-start.2 = (f32[768,768]{1,0:T(8,128)}, f32[768,768]{1,0:T(8,128)S(1)}, u32[]{:S(2)}, u32[]{:S(2)}) collective-permute-start(f32[768,768]{1,0:T(8,128)} %select_bitcast_fusion), channel_id=1, source_target_pairs={{0,16},{4,20},{8,24},{12,28},{16,0},{20,4},{24,8},{28,12},{1,17},{... | collective-permute-start | bytes 7077896 | tf_op jit(solution)/shard_map/ppermute | solution.py:10
Sparse Core Ops, SparseCore 0:
  12.5 58.3 all-reduce.1
where the time goes:
time: 347 us; the launch traced here: 346 us
  waiting for transfers between devices  251 us (72%)
  local copies, waits for them, and re-layouts  45.1 us (13%)
  other arithmetic  26.7 us (8%)
  between operations  14.2 us (4%)
  starting transfers between devices  5.37 us (2%)
  matrix products  3.73 us (1%)
    ppermute x3, waiting for transfers between devices, from_partner(): lax.ppermute(array, axis, [(i, i ^ 1 << stride) for i in range(lax.axis_s...  196 us
    psum x1, waiting for transfers between devices, local(): schur_remainder_patch = lax.psum(schur_remainder_patch, 'mode')  54.3 us
    transpose x6, other arithmetic, relabel_equations(): return jnp.take(rows_first.T, arrangement_list, axis=0).T  16.5 us
    gather x4, local copies, waits for them, and re-layouts, relabel_equations(): return jnp.take(rows_first.T, arrangement_list, axis=0).T  12.4 us
    gather x3, local copies, waits for them, and re-layouts, relabel_equations(): rows_first = jnp.take(schur_remainder_patch, arrangement_list, axis=0)  12.1 us
    gather x3, local copies, waits for them, and re-layouts, select_permutation(): return jnp.take(base_perm, shifted)  9.56 us
  transfers between devices with their start and end apart: 4, of which 4 were waited for; matrix products, arithmetic and copies ran while one was open for 3% of the time, Pallas kernels for 0%

commit v1 on v0

v1 whole, which is shorter than its diff:
```python
import functools
import math

import jax
import jax.numpy as jnp
from jax import lax
from jax.experimental import pallas as pl
from jax.experimental.pallas import tpu as pltpu
from jax.sharding import PartitionSpec as P

MESH = pl.DeviceIdType.MESH
NT = (((1,), (1,)), ((), ()))
LANES = 128


def plan(subs, modes):
    if subs == 8 and modes == 4:
        x, y, near, far = ("mode", 1), ("sub", 0), ("sub", 1), ("sub", 2)
        return [
            [(True, *x), (True, *y), (True, *near), (True, *far)],
            [(True, *y), (True, *near), (True, *far), (False, *x)],
            [(True, *near), (True, *x), (True, *y), (True, *far)],
        ], 2
    sub_bits, mode_bits = subs.bit_length() - 1, modes.bit_length() - 1
    steps = [(True, "sub", b) for b in range(sub_bits)]
    steps += [(False, "mode", b) for b in range(1, mode_bits)]
    return [steps] * 3, 1


def bit_of(value, bit):
    return (value // 2**bit) % 2


def body(subs, modes, parts, pieces, *refs):
    panels_ref, eig_ref, counts_ref, diag_ref, tables_ref, out_ref = refs[:6]
    wt, pt, to_core, from_core, fin, core_sems, fin_sems, cross_sems, send_sems, recv_sems = refs[6:16]
    steps = len(parts[0])
    accs = refs[16 : 16 + steps + 1]
    lands = refs[16 + steps + 1 :]
    count = len(parts)
    sub_me, mode_me = lax.axis_index("sub"), lax.axis_index("mode")
    core_me = mode_me % 2
    sep = panels_ref.shape[1]
    depth = panels_ref.shape[0]
    rows = sep // subs // pieces
    place = {"sub": sub_me, "mode": mode_me}

    def partner(axis, bit):
        here = place[axis]
        other = here + 2**bit * (1 - 2 * bit_of(here, bit))
        return (other, mode_me) if axis == "sub" else (sub_me, other)

    sibling = partner("mode", 0)
    links = sorted({step[1:] for part in parts for step in part} | {("mode", 0)})
    barrier = pltpu.get_barrier_semaphore()
    for axis, bit in links:
        pl.semaphore_signal(barrier, inc=1, device_id=partner(axis, bit), device_id_type=MESH)

    lanes = lax.broadcasted_iota(jnp.int32, (sep, sep), 1).astype(jnp.float32)
    first = lax.broadcasted_iota(jnp.int32, (sep, 1), 0).astype(jnp.float32)
    high_row = lax.broadcasted_iota(jnp.int32, (16, sep), 0) == 0

    def one_hot(index):
        return jnp.where(index == lanes, 1.0, 0.0).astype(jnp.bfloat16)

    index = first
    for level in reversed(range(subs.bit_length() - 1)):
        shifted = index + float(97 * level % sep)
        shifted = jnp.where(shifted >= sep, shifted - sep, shifted)
        row = tables_ref[pl.ds((sub_me // 2**level) * 2**level + 2**level - 1, 1), :]
        digits = jnp.where(high_row, row // 16, row % 16).astype(jnp.float32).astype(jnp.bfloat16)
        found = lax.dot_general(one_hot(shifted), digits, NT, preferred_element_type=jnp.float32)
        index = found[:, 0:1] * 16.0 + found[:, 1:2]
    moved = one_hot(index)

    live = lax.broadcasted_iota(jnp.int32, (1, depth), 1) + mode_me * depth < counts_ref[0]
    scale = jnp.where(live, 1.0, 0.0) / eig_ref[...]
    panels_t = lax.dot_general(moved, panels_ref[...], NT, preferred_element_type=jnp.float32)
    pt[...] = panels_t.astype(jnp.bfloat16)
    wt[...] = (panels_t * scale).astype(jnp.bfloat16)

    diag = diag_ref[...] * jnp.where(mode_me == 0, 1.0, 0.0)
    top = diag.astype(jnp.bfloat16).astype(jnp.float32)
    middle = (diag - top).astype(jnp.bfloat16).astype(jnp.float32)
    low = diag - top - middle
    pick = lax.broadcasted_iota(jnp.int32, (16, sep), 0)
    split = jnp.where(pick == 0, top, jnp.where(pick == 1, middle, jnp.where(pick == 2, low, 0.0)))
    got = lax.dot_general(moved, split.astype(jnp.bfloat16), NT, preferred_element_type=jnp.float32)
    diag_moved = got[:, 0:1] + got[:, 1:2] + got[:, 2:3]
    columns = lax.broadcasted_iota(jnp.int32, (sep, LANES), 1).astype(jnp.float32)

    def tile(core, p):
        start = pl.multiple_of((core * count + p) * LANES, LANES)
        product = lax.dot_general(
            wt[...], pt[pl.ds(start, LANES), :], NT, preferred_element_type=jnp.float32
        )
        on_diag = columns + start.astype(jnp.float32) == first
        return jnp.where(on_diag, diag_moved, 0.0) - product

    def slot_of(p, block):
        slot, taken = 0, 0
        for halve, axis, bit in parts[p]:
            if halve:
                if axis == "sub":
                    far = (bit_of(block // pieces, bit) + bit_of(sub_me, bit)) % 2
                else:
                    far = (bit_of(block % pieces, bit - 1) + bit_of(mode_me, bit)) % 2
                    taken = 1
                slot = slot * 2 + far
        return slot if taken else slot * pieces + block % pieces

    def core_copy(p):
        return pltpu.make_async_remote_copy(
            to_core.at[p], from_core.at[p], core_sems.at[0, p], core_sems.at[1, p], sibling, MESH
        )

    blocks = subs * pieces
    for p in range(count):
        value = tile(1 - core_me, p)
        for b in range(blocks):
            to_core[p, slot_of(p, b), :, :] = value[b * rows : (b + 1) * rows]
        if p == 0:
            pl.semaphore_wait(barrier, len(links))
        core_copy(p).start()

    sizes = []
    for p in range(count):
        n, own = blocks, []
        for halve, _, _ in parts[p]:
            n = n // 2 if halve else n
            own.append(n)
        sizes.append(own)

    def exchange(p, k):
        halve, axis, bit = parts[p][k]
        n = sizes[p][k]
        return pltpu.make_async_remote_copy(
            accs[k].at[p, pl.ds(n if halve else 0, n)],
            lands[k].at[p, pl.ds(0, n)],
            send_sems.at[p, k],
            recv_sems.at[p, k],
            partner(axis, bit),
            MESH,
        )

    for p in range(count):
        value = tile(core_me, p)
        for b in range(blocks):
            accs[0][p, slot_of(p, b), :, :] = value[b * rows : (b + 1) * rows]
    for p in range(count):
        core_copy(p).wait_recv()
        accs[0][p] = accs[0][p] + from_core[p]
        exchange(p, 0).start()

    cut = [any(halve and axis == "mode" for halve, axis, _ in part) for part in parts]
    piece_me = bit_of(mode_me, 1)

    def cross_copy(p):
        spot = fin.at[core_me, p, pl.ds(piece_me, 1)]
        return pltpu.make_async_remote_copy(
            spot, spot, cross_sems.at[0, p], cross_sems.at[1, p], partner("mode", 1), MESH
        )

    def final_copy(p):
        spot = fin.at[core_me, p]
        return pltpu.make_async_remote_copy(
            spot, spot, fin_sems.at[0, p], fin_sems.at[1, p], sibling, MESH
        )

    for k in range(steps):
        for p in range(count):
            n = sizes[p][k]
            exchange(p, k).wait_recv()
            total = accs[k][p, 0:n] + lands[k][p, 0:n]
            if k < steps - 1:
                accs[k + 1][p, 0:n] = total
                exchange(p, k + 1).start()
            elif cut[p]:
                fin[core_me, p, pl.ds(piece_me, 1)] = total
                cross_copy(p).start()
            else:
                fin[core_me, p] = total
                final_copy(p).start()
    for p in range(count):
        if cut[p]:
            cross_copy(p).wait_recv()
            final_copy(p).start()
    for p in range(count):
        final_copy(p).wait_recv()
    for c in range(2):
        for p in range(count):
            at = (c * count + p) * LANES
            for piece in range(pieces):
                out_ref[piece * rows : (piece + 1) * rows, at : at + LANES] = fin[c, p, piece]
    for p in range(count):
        core_copy(p).wait_send()
        for k in range(steps):
            exchange(p, k).wait_send()
        if cut[p]:
            cross_copy(p).wait_send()
        final_copy(p).wait_send()


def solution(mesh):
    subs, modes = mesh.shape["sub"], mesh.shape["mode"]
    parts, pieces = plan(subs, modes)

    def local(panels, eigvals, counts, separator_diag, tables):
        sep, depth = panels.shape[2], panels.shape[1]
        own = sep // subs
        rows = own // pieces
        count, steps, blocks = len(parts), len(parts[0]), subs * pieces
        f32 = jnp.float32

        def room(k):
            most = 0
            for part in parts:
                n = blocks
                for halve, _, _ in part[:k]:
                    n = n // 2 if halve else n
                most = max(most, n)
            return pltpu.VMEM((count, most, rows, LANES), f32)

        dma = pltpu.SemaphoreType.DMA
        root = pl.pallas_call(
            functools.partial(body, subs, modes, parts, pieces),
            out_shape=jax.ShapeDtypeStruct((own, sep), f32),
            in_specs=[
                pl.BlockSpec(memory_space=pltpu.VMEM),
                pl.BlockSpec(memory_space=pltpu.VMEM),
                pl.BlockSpec(memory_space=pltpu.SMEM),
                pl.BlockSpec(memory_space=pltpu.VMEM),
                pl.BlockSpec(memory_space=pltpu.VMEM),
            ],
            out_specs=pl.BlockSpec(memory_space=pltpu.VMEM),
            scratch_shapes=[
                pltpu.VMEM((sep, depth), jnp.bfloat16),
                pltpu.VMEM((sep, depth), jnp.bfloat16),
                pltpu.VMEM((count, blocks, rows, LANES), f32),
                pltpu.VMEM((count, blocks, rows, LANES), f32),
                pltpu.VMEM((2, count, pieces, rows, LANES), f32),
                dma((2, count)),
                dma((2, count)),
                dma((2, count)),
                dma((count, steps)),
                dma((count, steps)),
                *[room(k) for k in range(steps + 1)],
                *[room(k + 1) for k in range(steps)],
            ],
            compiler_params=pltpu.CompilerParams(
                collective_id=0, has_side_effects=True, vmem_limit_bytes=48 * 2**20
            ),
        )(panels[0], eigvals, counts, separator_diag, tables)
        return root * (1.0 / math.sqrt(subs))

    return jax.shard_map(
        local,
        mesh=mesh,
        in_specs=(P("sub", "mode", None), P("sub", "mode"), P("sub"), P("sub", None), P()),
        out_specs=P("sub", None),
        check_vma=False,
    )
```

time: 347 us -> 35.6 us (0.10)
  waiting for transfers between devices: 251 us -> 0 us
  local copies, waits for them, and re-layouts: 45.1 us -> 2.57 us
  Pallas kernels: 0 us -> 31.4 us
  other arithmetic: 26.7 us -> 0.74 us
  between operations: 14.2 us -> 0.68 us
  starting transfers between devices: 5.37 us -> 0 us
  matrix products: 3.73 us -> 0 us
    ppermute x3 -> x0, waiting for transfers between devices: 196 us -> none  [from_partner(): lax.ppermute(array, axis, [(i, i ^ 1 << stride) for i in range(lax.axis_s...]
    psum x1 -> x0, waiting for transfers between devices: 54.3 us -> none  [local(): schur_remainder_patch = lax.psum(schur_remainder_patch, 'mode')]
    gather x10 -> x0, local copies, waits for them, and re-layouts: 34 us -> none  [the longest x4 12.4 us: relabel_equations(): return jnp.take(rows_first.T, arrangement_list, axis=0).T]
    pallas_call x0 -> x1, Pallas kernels: none -> 31.4 us  [local(): pl.pallas_call(functools.partial(body, subs, modes, parts, pieces), out_s...]
    transpose x6 -> x0, other arithmetic: 16.5 us -> none  [relabel_equations(): return jnp.take(rows_first.T, arrangement_list, axis=0).T]
    add x2 -> x0, other arithmetic: 6.92 us -> none  [local(): schur_remainder_patch + from_partner(schur_remainder_patch, 'sub', bit_po...]
    transpose x3 -> x0, local copies, waits for them, and re-layouts: 6.1 us -> none  [relabel_equations(): return jnp.take(rows_first.T, arrangement_list, axis=0).T]
    ppermute x3 -> x0, starting transfers between devices: 5.37 us -> none  [from_partner(): lax.ppermute(array, axis, [(i, i ^ 1 << stride) for i in range(lax.axis_s...]
  transfers between devices with their start and end apart: 4 -> 0, of which waited for: 4 -> 0; matrix products, arithmetic and copies ran while one was open for 3% -> 0% of each run, Pallas kernels for 0% -> 0%
where the time goes in v1:
time: 35.6 us; the launch traced here: 35.4 us
  Pallas kernels  31.4 us (88%)
  local copies, waits for them, and re-layouts  2.57 us (7%)
  other arithmetic  0.74 us (2%)
  between operations  0.68 us (2%)
    pallas_call x1, Pallas kernels, local(): pl.pallas_call(functools.partial(body, subs, modes, parts, pieces), out_s...  31.4 us
    unnamed x8, local copies, waits for them, and re-layouts  2.57 us
    mul x1, other arithmetic, local(): return root * (1.0 / math.sqrt(subs))  0.74 us

profile of v1, /device:TPU:0, one launch (start us, length us, event | category | flops | bytes accessed | tf_op | source)
XLA Modules:
  0.0 35.4 jit_solution(2008834108691814599)
XLA Ops:
  0.0 0.0 copy-start.2
  0.7 0.0 copy-done.2
  0.7 0.0 copy-start
  0.7 1.1 %copy-done = bf16[1,512,768]{2,1,0:T(8,128)(2,1)S(1)} copy-done((bf16[1,512,768]{2,1,0:T(8,128)(2,1)S(1)}, bf16[1,512,768]{2,1,0:T(8,128)(2,1)}, u32[]{:S(2)}) %copy-start) | copy-done | bytes 786456
  1.8 0.0 copy-start.1
  1.8 0.7 %copy-done.1 = s32[8,768]{1,0:T(8,128)S(1)} copy-done((s32[8,768]{1,0:T(8,128)S(1)}, s32[8,768]{1,0:T(8,128)}, u32[]{:S(2)}) %copy-start.1) | copy-done | bytes 24600
  2.6 0.0 copy-start.3
  2.6 0.7 %copy-done.3 = f32[1,512]{1,0:T(1,128)S(1)} copy-done((f32[1,512]{1,0:T(1,128)S(1)}, f32[1,512]{1,0:T(1,128)}, u32[]{:S(2)}) %copy-start.3) | copy-done | bytes 2072
  3.2 31.4 %shard_map.55 = f32[96,768]{1,0:T(8,128)S(1)} custom-call(bf16[512,768]{1,0:T(8,128)(2,1)S(1)} %bitcast.1, f32[1,512]{1,0:T(1,128)S(1)} %copy-done.3, s32[1]{0:T(128)S(6)} %copy.6.refs_2_, f32[1,768]{1,0:T(1,128)S(1)} %copy-done.2, s32[8,768]{1,0:T(8,128)S(1)} %copy-done.1), custom_call_target="tpu_custom_call" | custom-call | tf_op jit(solution)/shard_map/pallas_call | solution.py:225
  34.6 0.7 %broadcast_multiply_fusion = f32[96,768]{1,0:T(8,128)} fusion(f32[96,768]{1,0:T(8,128)S(1)} %shard_map.55), kind=kLoop, calls=%fused_computation | loop fusion | flops 73728 | bytes 589824 | tf_op jit(solution)/shard_map/mul | solution.py:254
Async XLA Ops:
  0.0 0.7 %copy-start.2 = (f32[1,768]{1,0:T(1,128)S(1)}, f32[1,768]{1,0:T(1,128)}, u32[]{:S(2)}) copy-start(f32[1,768]{1,0:T(1,128)} %refs_3_.1) | copy-start | bytes 9220
  0.7 1.1 %copy-start = (bf16[1,512,768]{2,1,0:T(8,128)(2,1)S(1)}, bf16[1,512,768]{2,1,0:T(8,128)(2,1)}, u32[]{:S(2)}) copy-start(bf16[1,512,768]{2,1,0:T(8,128)(2,1)} %param.5) | copy-start | bytes 2359300
  1.8 0.7 %copy-start.1 = (s32[8,768]{1,0:T(8,128)S(1)}, s32[8,768]{1,0:T(8,128)}, u32[]{:S(2)}) copy-start(s32[8,768]{1,0:T(8,128)} %refs_4_.1) | copy-start | bytes 73732
  2.6 0.7 %copy-start.3 = (f32[1,512]{1,0:T(1,128)S(1)}, f32[1,512]{1,0:T(1,128)}, u32[]{:S(2)}) copy-start(f32[1,512]{1,0:T(1,128)} %refs_1_.1) | copy-start | bytes 6148

commit v2 on v1

v2 whole, which is shorter than its diff:
```python
import functools
import math

import jax
import jax.numpy as jnp
from jax import lax
from jax.experimental import pallas as pl
from jax.experimental.pallas import tpu as pltpu
from jax.sharding import PartitionSpec as P

MESH = pl.DeviceIdType.MESH
NT = (((1,), (1,)), ((), ()))
LANES = 128


def plan(subs, modes):
    if subs == 8 and modes == 4:
        x, y, near, far = ("mode", 1), ("sub", 0), ("sub", 1), ("sub", 2)
        return [
            [(True, *x), (True, *y), (True, *near), (True, *far)],
            [(True, *y), (True, *near), (True, *far), (False, *x)],
            [(True, *near), (True, *x), (True, *y), (True, *far)],
        ], 2, 2
    sub_bits, mode_bits = subs.bit_length() - 1, modes.bit_length() - 1
    steps = [(True, "sub", b) for b in range(sub_bits)]
    steps += [(False, "mode", b) for b in range(1, mode_bits)]
    return [steps] * 3, 1, 1


def bit_of(value, bit):
    return (value // 2**bit) % 2


def body(subs, modes, column_parts, pieces, shares, *refs):
    panels_hbm, eig_hbm, counts_ref, diag_hbm, tables_hbm, out_ref = refs[:6]
    panels_ref, eig_ref, diag_ref, tables_ref, load_sems = refs[-5:]
    wt, pt, to_core, from_core, fin, core_sems, fin_sems, send_sems, recv_sems = refs[6:15]
    parts = [part for part in column_parts for _ in range(shares)]
    order = [q * shares + h for h in range(shares) for q in range(len(column_parts))]
    steps = len(parts[0])
    accs = refs[15 : 15 + steps + 1]
    lands = refs[15 + steps + 1 : -5]
    count, chunks = len(parts), len(column_parts)
    loads = [
        pltpu.make_async_copy(source, kept, load_sems.at[i])
        for i, (source, kept) in enumerate(
            [
                (tables_hbm, tables_ref),
                (panels_hbm, panels_ref),
                (eig_hbm, eig_ref),
                (diag_hbm, diag_ref),
            ]
        )
    ]
    for load in loads:
        load.start()
    sub_me, mode_me = lax.axis_index("sub"), lax.axis_index("mode")
    core_me = mode_me % 2
    sep = panels_ref.shape[1]
    depth = panels_ref.shape[0]
    rows = sep // subs // pieces // shares
    place = {"sub": sub_me, "mode": mode_me}

    def partner(axis, bit):
        here = place[axis]
        other = here + 2**bit * (1 - 2 * bit_of(here, bit))
        return (other, mode_me) if axis == "sub" else (sub_me, other)

    sibling = partner("mode", 0)
    links = sorted({step[1:] for part in parts for step in part} | {("mode", 0)})
    barrier = pltpu.get_barrier_semaphore()
    for axis, bit in links:
        pl.semaphore_signal(barrier, inc=1, device_id=partner(axis, bit), device_id_type=MESH)

    first = lax.broadcasted_iota(jnp.int32, (sep, 1), 0)
    across = (sub_me, partner("mode", 1)[1] + 1 - 2 * core_me) if pieces == 2 else None
    greeted = len(links) + (pieces == 2)
    if pieces == 2:
        pl.semaphore_signal(barrier, inc=1, device_id=across, device_id_type=MESH)

    runs = sep // LANES
    place_in_run = lax.broadcasted_iota(jnp.int32, (LANES, sep), 0)
    run_row = lax.broadcasted_iota(jnp.int32, (8, sep), 0)
    run_of = lax.broadcasted_iota(jnp.int32, (8, LANES), 0)
    loads[0].wait()
    index = lax.broadcasted_iota(jnp.int32, (1, sep), 1)
    for level in reversed(range(subs.bit_length() - 1)):
        index = index + 97 * level % sep
        index = jnp.where(index >= sep, index - sep, index)
        line = (sub_me // 2**level) * 2**level + 2**level - 1
        row = tables_ref[pl.ds(line, 1), :]
        table = jnp.zeros((8, LANES), jnp.int32)
        for run in range(runs):
            table = jnp.where(run_of == run, row[:, run * LANES : (run + 1) * LANES], table)
        digits = jnp.concatenate([table // 16, table % 16], axis=0).astype(jnp.float32).astype(jnp.bfloat16)
        mark = jnp.where(place_in_run == index % LANES, 1.0, 0.0).astype(jnp.bfloat16)
        found = jnp.dot(digits, mark, preferred_element_type=jnp.float32)
        value = jnp.where(run_row == index // LANES, found[0:8] * 16.0 + found[8:16], 0.0)
        index = jnp.sum(value, axis=0, keepdims=True).astype(jnp.int32)
    target = jnp.broadcast_to(index, (8, sep)).T[:, 0:1]
    lanes = lax.broadcasted_iota(jnp.int32, (sep, sep), 1)
    moved = jnp.where(target == lanes, 1.0, 0.0).astype(jnp.bfloat16)

    for load in loads[1:]:
        load.wait()
    live = lax.broadcasted_iota(jnp.int32, (1, depth), 1) + mode_me * depth < counts_ref[0]
    scale = jnp.where(live, 1.0, 0.0) / eig_ref[...]
    panels_t = lax.dot_general(moved, panels_ref[...], NT, preferred_element_type=jnp.float32)
    pt[...] = panels_t.astype(jnp.bfloat16)
    wt[...] = (panels_t * scale).astype(jnp.bfloat16)

    diag = diag_ref[...] * jnp.where(mode_me == 0, 1.0, 0.0)
    top = diag.astype(jnp.bfloat16).astype(jnp.float32)
    middle = (diag - top).astype(jnp.bfloat16).astype(jnp.float32)
    low = diag - top - middle
    pick = lax.broadcasted_iota(jnp.int32, (16, sep), 0)
    split = jnp.where(pick == 0, top, jnp.where(pick == 1, middle, jnp.where(pick == 2, low, 0.0)))
    got = lax.dot_general(moved, split.astype(jnp.bfloat16), NT, preferred_element_type=jnp.float32)
    diag_moved = got[:, 0:1] + got[:, 1:2] + got[:, 2:3]
    columns = lax.broadcasted_iota(jnp.int32, (sep, LANES), 1)

    def tile(core, p):
        start = pl.multiple_of((core * chunks + p) * LANES, LANES)
        product = lax.dot_general(
            wt[...], pt[pl.ds(start, LANES), :], NT, preferred_element_type=jnp.float32
        )
        on_diag = columns + start == first
        return jnp.where(on_diag, diag_moved, 0.0) - product

    def slot_of(p, block):
        slot, taken = 0, 0
        for halve, axis, bit in parts[p]:
            if halve:
                if axis == "sub":
                    far = (bit_of(block // pieces, bit) + bit_of(sub_me, bit)) % 2
                else:
                    far = (bit_of(block % pieces, bit - 1) + bit_of(mode_me, bit)) % 2
                    taken = 1
                slot = slot * 2 + far
        return slot if taken else slot * pieces + block % pieces

    def core_copy(p):
        return pltpu.make_async_remote_copy(
            to_core.at[p], from_core.at[p], core_sems.at[0, p], core_sems.at[1, p], sibling, MESH
        )

    blocks = subs * pieces
    def store_tile(kept, core, chunk):
        value = tile(core, chunk)
        for b in range(blocks):
            slot = slot_of(chunk * shares, b)
            for h in range(shares):
                at = (b * shares + h) * rows
                kept[chunk * shares + h, slot, :, :] = value[at : at + rows]

    for chunk in range(chunks):
        store_tile(to_core, 1 - core_me, chunk)
        if chunk == 0:
            pl.semaphore_wait(barrier, greeted)
        for h in range(shares):
            core_copy(chunk * shares + h).start()

    sizes = []
    for p in range(count):
        n, own = blocks, []
        for halve, _, _ in parts[p]:
            n = n // 2 if halve else n
            own.append(n)
        sizes.append(own)

    def exchange(p, k):
        halve, axis, bit = parts[p][k]
        n = sizes[p][k]
        return pltpu.make_async_remote_copy(
            accs[k].at[p, pl.ds(n if halve else 0, n)],
            lands[k].at[p, pl.ds(0, n)],
            send_sems.at[p, k],
            recv_sems.at[p, k],
            partner(axis, bit),
            MESH,
        )

    for chunk in range(chunks):
        store_tile(accs[0], core_me, chunk)
    for p in order:
        core_copy(p).wait_recv()
        accs[0][p] = accs[0][p] + from_core[p]
        exchange(p, 0).start()

    cut = [any(halve and axis == "mode" for halve, axis, _ in part) for part in parts]
    piece_me = bit_of(mode_me, 1)

    def last_copies(p):
        spot = fin.at[core_me, p, pl.ds(piece_me, 1)] if cut[p] else fin.at[core_me, p]
        targets = [sibling, partner("mode", 1), across] if cut[p] else [sibling]
        return [
            pltpu.make_async_remote_copy(spot, spot, fin_sems.at[0, p, i], fin_sems.at[1, p, i], target, MESH)
            for i, target in enumerate(targets)
        ]

    for k in range(steps):
        for p in order:
            n = sizes[p][k]
            exchange(p, k).wait_recv()
            total = accs[k][p, 0:n] + lands[k][p, 0:n]
            if k < steps - 1:
                accs[k + 1][p, 0:n] = total
                exchange(p, k + 1).start()
                continue
            if cut[p]:
                fin[core_me, p, pl.ds(piece_me, 1)] = total
            else:
                fin[core_me, p] = total
            for copy in last_copies(p):
                copy.start()
    for p in order:
        for copy in last_copies(p):
            copy.wait_recv()
    for c in range(2):
        for p in range(count):
            at = (c * chunks + p // shares) * LANES
            for piece in range(pieces):
                down = (piece * shares + p % shares) * rows
                out_ref[down : down + rows, at : at + LANES] = fin[c, p, piece]
    for p in range(count):
        core_copy(p).wait_send()
        for k in range(steps):
            exchange(p, k).wait_send()
        for copy in last_copies(p):
            copy.wait_send()


def solution(mesh):
    subs, modes = mesh.shape["sub"], mesh.shape["mode"]
    column_parts, pieces, shares = plan(subs, modes)
    parts = [part for part in column_parts for _ in range(shares)]

    def local(panels, eigvals, counts, separator_diag, tables):
        sep, depth = panels.shape[2], panels.shape[1]
        own = sep // subs
        rows = own // pieces // shares
        count, steps, blocks = len(parts), len(parts[0]), subs * pieces
        f32 = jnp.float32

        def room(k):
            most = 0
            for part in parts:
                n = blocks
                for halve, _, _ in part[:k]:
                    n = n // 2 if halve else n
                most = max(most, n)
            return pltpu.VMEM((count, most, rows, LANES), f32)

        dma = pltpu.SemaphoreType.DMA
        root = pl.pallas_call(
            functools.partial(body, subs, modes, column_parts, pieces, shares),
            out_shape=jax.ShapeDtypeStruct((own, sep), f32),
            in_specs=[
                pl.BlockSpec(memory_space=pltpu.HBM),
                pl.BlockSpec(memory_space=pltpu.HBM),
                pl.BlockSpec(memory_space=pltpu.SMEM),
                pl.BlockSpec(memory_space=pltpu.HBM),
                pl.BlockSpec(memory_space=pltpu.HBM),
            ],
            out_specs=pl.BlockSpec(memory_space=pltpu.VMEM),
            scratch_shapes=[
                pltpu.VMEM((sep, depth), jnp.bfloat16),
                pltpu.VMEM((sep, depth), jnp.bfloat16),
                pltpu.VMEM((count, blocks, rows, LANES), f32),
                pltpu.VMEM((count, blocks, rows, LANES), f32),
                pltpu.VMEM((2, count, pieces, rows, LANES), f32),
                dma((2, count)),
                dma((2, count, 3)),
                dma((count, steps)),
                dma((count, steps)),
                *[room(k) for k in range(steps + 1)],
                *[room(k + 1) for k in range(steps)],
                pltpu.VMEM((depth, sep), panels.dtype),
                pltpu.VMEM(eigvals.shape, f32),
                pltpu.VMEM(separator_diag.shape, f32),
                pltpu.VMEM(tables.shape, tables.dtype),
                dma((4,)),
            ],
            compiler_params=pltpu.CompilerParams(
                collective_id=0, has_side_effects=True, vmem_limit_bytes=48 * 2**20
            ),
        )(panels[0], eigvals, counts, separator_diag, tables)
        return root * (1.0 / math.sqrt(subs))

    return jax.shard_map(
        local,
        mesh=mesh,
        in_specs=(P("sub", "mode", None), P("sub", "mode"), P("sub"), P("sub", None), P()),
        out_specs=P("sub", None),
        check_vma=False,
    )
```

time: 35.6 us -> 32.4 us (0.910)
  Pallas kernels: 31.4 us -> 28.1 us
    pallas_call x1, Pallas kernels: 31.4 us -> 28.1 us  [local(): pl.pallas_call(functools.partial(body, subs, modes, column_parts, pieces,...]
where the time goes in v2:
time: 32.4 us; the launch traced here: 32.1 us
  Pallas kernels  28.1 us (87%)
  local copies, waits for them, and re-layouts  2.57 us (8%)
  other arithmetic  0.74 us (2%)
  between operations  0.68 us (2%)
    pallas_call x1, Pallas kernels, local(): pl.pallas_call(functools.partial(body, subs, modes, column_parts, pieces,...  28.1 us
    unnamed x8, local copies, waits for them, and re-layouts  2.57 us
    mul x1, other arithmetic, local(): return root * (1.0 / math.sqrt(subs))  0.74 us

profile of v2, /device:TPU:0, one launch (start us, length us, event | category | flops | bytes accessed | tf_op | source)
XLA Modules:
  0.0 32.1 jit_solution(3670401613136614131)
XLA Ops:
  0.0 0.0 copy-start.2
  0.7 0.0 copy-done.2
  0.7 0.0 copy-start
  0.7 1.1 %copy-done = bf16[1,512,768]{2,1,0:T(8,128)(2,1)S(1)} copy-done((bf16[1,512,768]{2,1,0:T(8,128)(2,1)S(1)}, bf16[1,512,768]{2,1,0:T(8,128)(2,1)}, u32[]{:S(2)}) %copy-start) | copy-done | bytes 786456
  1.8 0.0 copy-start.1
  1.8 0.7 %copy-done.1 = s32[8,768]{1,0:T(8,128)S(1)} copy-done((s32[8,768]{1,0:T(8,128)S(1)}, s32[8,768]{1,0:T(8,128)}, u32[]{:S(2)}) %copy-start.1) | copy-done | bytes 24600
  2.6 0.0 copy-start.3
  2.6 0.7 %copy-done.3 = f32[1,512]{1,0:T(1,128)S(1)} copy-done((f32[1,512]{1,0:T(1,128)S(1)}, f32[1,512]{1,0:T(1,128)}, u32[]{:S(2)}) %copy-start.3) | copy-done | bytes 2072
  3.2 28.1 %shard_map.55 = f32[96,768]{1,0:T(8,128)S(1)} custom-call(bf16[512,768]{1,0:T(8,128)(2,1)S(1)} %bitcast.1, f32[1,512]{1,0:T(1,128)S(1)} %copy-done.3, s32[1]{0:T(128)S(6)} %copy.6.refs_2_, f32[1,768]{1,0:T(1,128)S(1)} %copy-done.2, s32[8,768]{1,0:T(8,128)S(1)} %copy-done.1), custom_call_target="tpu_custom_call" | custom-call | tf_op jit(solution)/shard_map/pallas_call | solution.py:255
  31.4 0.7 %broadcast_multiply_fusion = f32[96,768]{1,0:T(8,128)} fusion(f32[96,768]{1,0:T(8,128)S(1)} %shard_map.55), kind=kLoop, calls=%fused_computation | loop fusion | flops 73728 | bytes 589824 | tf_op jit(solution)/shard_map/mul | solution.py:288
Async XLA Ops:
  0.0 0.7 %copy-start.2 = (f32[1,768]{1,0:T(1,128)S(1)}, f32[1,768]{1,0:T(1,128)}, u32[]{:S(2)}) copy-start(f32[1,768]{1,0:T(1,128)} %refs_3_.1) | copy-start | bytes 9220
  0.7 1.1 %copy-start = (bf16[1,512,768]{2,1,0:T(8,128)(2,1)S(1)}, bf16[1,512,768]{2,1,0:T(8,128)(2,1)}, u32[]{:S(2)}) copy-start(bf16[1,512,768]{2,1,0:T(8,128)(2,1)} %param.5) | copy-start | bytes 2359300
  1.8 0.7 %copy-start.1 = (s32[8,768]{1,0:T(8,128)S(1)}, s32[8,768]{1,0:T(8,128)}, u32[]{:S(2)}) copy-start(s32[8,768]{1,0:T(8,128)} %refs_4_.1) | copy-start | bytes 73732
  2.6 0.7 %copy-start.3 = (f32[1,512]{1,0:T(1,128)S(1)}, f32[1,512]{1,0:T(1,128)}, u32[]{:S(2)}) copy-start(f32[1,512]{1,0:T(1,128)} %refs_1_.1) | copy-start | bytes 6148

commit v3 on v2

--- a/solution.py
+++ b/solution.py
@@ -104,28 +104,21 @@
     for load in loads[1:]:
         load.wait()
     live = lax.broadcasted_iota(jnp.int32, (1, depth), 1) + mode_me * depth < counts_ref[0]
-    scale = jnp.where(live, 1.0, 0.0) / eig_ref[...]
+    minus_scale = jnp.where(live, -1.0, 0.0) / eig_ref[...]
     panels_t = lax.dot_general(moved, panels_ref[...], NT, preferred_element_type=jnp.float32)
     pt[...] = panels_t.astype(jnp.bfloat16)
-    wt[...] = (panels_t * scale).astype(jnp.bfloat16)
-
-    diag = diag_ref[...] * jnp.where(mode_me == 0, 1.0, 0.0)
-    top = diag.astype(jnp.bfloat16).astype(jnp.float32)
-    middle = (diag - top).astype(jnp.bfloat16).astype(jnp.float32)
-    low = diag - top - middle
-    pick = lax.broadcasted_iota(jnp.int32, (16, sep), 0)
-    split = jnp.where(pick == 0, top, jnp.where(pick == 1, middle, jnp.where(pick == 2, low, 0.0)))
-    got = lax.dot_general(moved, split.astype(jnp.bfloat16), NT, preferred_element_type=jnp.float32)
-    diag_moved = got[:, 0:1] + got[:, 1:2] + got[:, 2:3]
+    wt[...] = (panels_t * minus_scale).astype(jnp.bfloat16)
+
     columns = lax.broadcasted_iota(jnp.int32, (sep, LANES), 1)
 
     def tile(core, p):
         start = pl.multiple_of((core * chunks + p) * LANES, LANES)
-        product = lax.dot_general(
+        return lax.dot_general(
             wt[...], pt[pl.ds(start, LANES), :], NT, preferred_element_type=jnp.float32
         )
-        on_diag = columns + start == first
-        return jnp.where(on_diag, diag_moved, 0.0) - product
+
+    def on_diag(core, p):
+        return columns + (core * chunks + p) * LANES == first
 
     def slot_of(p, block):
         slot, taken = 0, 0
@@ -145,8 +138,7 @@
         )
 
     blocks = subs * pieces
-    def store_tile(kept, core, chunk):
-        value = tile(core, chunk)
+    def store_tile(kept, chunk, value):
         for b in range(blocks):
             slot = slot_of(chunk * shares, b)
             for h in range(shares):
@@ -154,7 +146,7 @@
                 kept[chunk * shares + h, slot, :, :] = value[at : at + rows]
 
     for chunk in range(chunks):
-        store_tile(to_core, 1 - core_me, chunk)
+        store_tile(to_core, chunk, tile(1 - core_me, chunk))
         if chunk == 0:
             pl.semaphore_wait(barrier, greeted)
         for h in range(shares):
@@ -180,8 +172,17 @@
             MESH,
         )
 
+    diag = diag_ref[...] * jnp.where(mode_me // 2 == 0, 1.0, 0.0)
+    top = diag.astype(jnp.bfloat16).astype(jnp.float32)
+    middle = (diag - top).astype(jnp.bfloat16).astype(jnp.float32)
+    low = diag - top - middle
+    pick = lax.broadcasted_iota(jnp.int32, (16, sep), 0)
+    split = jnp.where(pick == 0, top, jnp.where(pick == 1, middle, jnp.where(pick == 2, low, 0.0)))
+    got = lax.dot_general(moved, split.astype(jnp.bfloat16), NT, preferred_element_type=jnp.float32)
+    diag_moved = got[:, 0:1] + got[:, 1:2] + got[:, 2:3]
     for chunk in range(chunks):
-        store_tile(accs[0], core_me, chunk)
+        placed = jnp.where(on_diag(core_me, chunk), diag_moved, 0.0)
+        store_tile(accs[0], chunk, tile(core_me, chunk) + placed)
     for p in order:
         core_copy(p).wait_recv()
         accs[0][p] = accs[0][p] + from_core[p]

time: 32.4 us -> 32.4 us (level)
  no operation moved by 1% of the time
where the time goes in v3:
time: 32.4 us; the launch traced here: 32.2 us
  Pallas kernels  28.2 us (87%)
  local copies, waits for them, and re-layouts  2.57 us (8%)
  other arithmetic  0.74 us (2%)
  between operations  0.68 us (2%)
    pallas_call x1, Pallas kernels, local(): pl.pallas_call(functools.partial(body, subs, modes, column_parts, pieces,...  28.2 us
    unnamed x8, local copies, waits for them, and re-layouts  2.57 us
    mul x1, other arithmetic, local(): return root * (1.0 / math.sqrt(subs))  0.74 us

profile of v3, /device:TPU:0, one launch (start us, length us, event | category | flops | bytes accessed | tf_op | source)
XLA Modules:
  0.0 32.2 jit_solution(17492938787825301121)
XLA Ops:
  0.0 0.0 copy-start.2
  0.7 0.0 copy-done.2
  0.7 0.0 copy-start
  0.7 1.1 %copy-done = bf16[1,512,768]{2,1,0:T(8,128)(2,1)S(1)} copy-done((bf16[1,512,768]{2,1,0:T(8,128)(2,1)S(1)}, bf16[1,512,768]{2,1,0:T(8,128)(2,1)}, u32[]{:S(2)}) %copy-start) | copy-done | bytes 786456
  1.8 0.0 copy-start.1
  1.8 0.7 %copy-done.1 = s32[8,768]{1,0:T(8,128)S(1)} copy-done((s32[8,768]{1,0:T(8,128)S(1)}, s32[8,768]{1,0:T(8,128)}, u32[]{:S(2)}) %copy-start.1) | copy-done | bytes 24600
  2.6 0.0 copy-start.3
  2.6 0.7 %copy-done.3 = f32[1,512]{1,0:T(1,128)S(1)} copy-done((f32[1,512]{1,0:T(1,128)S(1)}, f32[1,512]{1,0:T(1,128)}, u32[]{:S(2)}) %copy-start.3) | copy-done | bytes 2072
  3.2 28.2 %shard_map.55 = f32[96,768]{1,0:T(8,128)S(1)} custom-call(bf16[512,768]{1,0:T(8,128)(2,1)S(1)} %bitcast.1, f32[1,512]{1,0:T(1,128)S(1)} %copy-done.3, s32[1]{0:T(128)S(6)} %copy.6.refs_2_, f32[1,768]{1,0:T(1,128)S(1)} %copy-done.2, s32[8,768]{1,0:T(8,128)S(1)} %copy-done.1), custom_call_target="tpu_custom_call" | custom-call | tf_op jit(solution)/shard_map/pallas_call | solution.py:256
  31.4 0.7 %broadcast_multiply_fusion = f32[96,768]{1,0:T(8,128)} fusion(f32[96,768]{1,0:T(8,128)S(1)} %shard_map.55), kind=kLoop, calls=%fused_computation | loop fusion | flops 73728 | bytes 589824 | tf_op jit(solution)/shard_map/mul | solution.py:289
Async XLA Ops:
  0.0 0.7 %copy-start.2 = (f32[1,768]{1,0:T(1,128)S(1)}, f32[1,768]{1,0:T(1,128)}, u32[]{:S(2)}) copy-start(f32[1,768]{1,0:T(1,128)} %refs_3_.1) | copy-start | bytes 9220
  0.7 1.1 %copy-start = (bf16[1,512,768]{2,1,0:T(8,128)(2,1)S(1)}, bf16[1,512,768]{2,1,0:T(8,128)(2,1)}, u32[]{:S(2)}) copy-start(bf16[1,512,768]{2,1,0:T(8,128)(2,1)} %param.5) | copy-start | bytes 2359300
  1.8 0.7 %copy-start.1 = (s32[8,768]{1,0:T(8,128)S(1)}, s32[8,768]{1,0:T(8,128)}, u32[]{:S(2)}) copy-start(s32[8,768]{1,0:T(8,128)} %refs_4_.1) | copy-start | bytes 73732
  2.6 0.7 %copy-start.3 = (f32[1,512]{1,0:T(1,128)S(1)}, f32[1,512]{1,0:T(1,128)}, u32[]{:S(2)}) copy-start(f32[1,512]{1,0:T(1,128)} %refs_1_.1) | copy-start | bytes 6148
